TPU v7x, 32 devices: a whole 2x2x4 slice. The times are simulated.
32 devices in a mesh: dp: 4 (over y, x), fsdp: 8 (over z, core).
Axes of the slice: x: 2, y: 2, z: 4, core: 2. Of those that a mesh axis runs over, the one named last changes fastest.
Arguments:
- states: bfloat16 [16384, 1024], P(('dp', 'fsdp')), may hold values from -6 to 6
- pad_mask: int32 [128, 128], P(('dp', 'fsdp')), may hold values from 0 to 1, as said below
- query_proj: bfloat16 [1024, 1024], P(('dp', 'fsdp')), may hold values from -0.1875 to 0.1875
- key_proj: bfloat16 [1024, 1024], P(('dp', 'fsdp')), may hold values from -0.1875 to 0.1875
- value_proj: bfloat16 [1024, 1024], P(('dp', 'fsdp')), may hold values from -0.1875 to 0.1875
- attn_proj: bfloat16 [1024, 1024], P(('dp', 'fsdp')), may hold values from -2 to 2
- query_bias: bfloat16 [1024], P(('dp', 'fsdp')), may hold values from -3 to 3
- value_bias: bfloat16 [1024], P(('dp', 'fsdp')), may hold values from -3 to 3
- attn_bias: bfloat16 [1024], P(('dp', 'fsdp')), may hold values from -3 to 3
- first_gain: bfloat16 [1024], P(('dp', 'fsdp')), may hold values from 0.5 to 1.5
- first_shift: bfloat16 [1024], P(('dp', 'fsdp')), may hold values from -3 to 3
- inner_proj: bfloat16 [1024, 4096], P(('dp', 'fsdp')), may hold values from -0.1875 to 0.1875
- inner_bias: bfloat16 [4096], P(('dp', 'fsdp')), may hold values from -3 to 3
- outer_proj: bfloat16 [4096, 1024], P(('dp', 'fsdp')), may hold values from -0.09375 to 0.09375
- outer_bias: bfloat16 [1024], P(('dp', 'fsdp')), may hold values from -3 to 3
- second_gain: bfloat16 [1024], P(('dp', 'fsdp')), may hold values from 0.5 to 1.5
- second_shift: bfloat16 [1024], P(('dp', 'fsdp')), may hold values from -3 to 3
- out_grad: bfloat16 [16384, 1024], P(('dp', 'fsdp')), may hold values from -6 to 6
Outputs:
- encoded: bfloat16 [16384, 1024], P(('dp', 'fsdp'))
- states_grad: float32 [16384, 1024], P(('dp', 'fsdp'))
- query_grad: float32 [1024, 1024], P(('dp', 'fsdp'))
- keys_grad: float32 [1024, 1024], P(('dp', 'fsdp'))
- values_grad: float32 [1024, 1024], P(('dp', 'fsdp'))
- attn_grad: float32 [1024, 1024], P(('dp', 'fsdp'))
- qbias_grad: float32 [1024], P(('dp', 'fsdp'))
- vbias_grad: float32 [1024], P(('dp', 'fsdp'))
- abias_grad: float32 [1024], P(('dp', 'fsdp'))
- fgain_grad: float32 [1024], P(('dp', 'fsdp'))
- fshift_grad: float32 [1024], P(('dp', 'fsdp'))
- inner_grad: float32 [1024, 4096], P(('dp', 'fsdp'))
- ibias_grad: float32 [4096], P(('dp', 'fsdp'))
- outer_grad: float32 [4096, 1024], P(('dp', 'fsdp'))
- obias_grad: float32 [1024], P(('dp', 'fsdp'))
- sgain_grad: float32 [1024], P(('dp', 'fsdp'))
- sshift_grad: float32 [1024], P(('dp', 'fsdp'))
Inputs may be any that keep to these rules, and one draw needn't show every extreme that they name: `pad_mask`: in each segment the ones form a prefix of 32 to 128 tokens.
All inputs are finite; a program needn't handle non-finite values.
Results may differ from a plain program's by a relative error of at most 0.014.
Values may be sent and summed in bfloat16 or wider, within the bound.
A program may use at most 256 MiB of HBM per device.

v0:
```python
import jax
import jax.numpy as jnp
from jax import lax
from jax.sharding import PartitionSpec as P

HEADS = 16
MICRO = 2


epsilon = 1e-05
neg_fill = -1e30


def normalize(hidden, gain, shift):
    center = hidden - jnp.mean(hidden, axis=-1, keepdims=True)
    spread = jnp.mean(center * center, axis=-1, keepdims=True)
    return center * lax.rsqrt(spread + epsilon) * gain + shift


def exact_gelu(value):
    return jax.nn.gelu(value, approximate=False)


def contract_rows(left, right):
    return lax.dot_general(
        left, right, (((0,), (0,)), ((), ())), preferred_element_type=jnp.float32
    )


def times_transposed(left, right):
    return lax.dot_general(
        left, right, (((1,), (1,)), ((), ())), preferred_element_type=jnp.float32
    )


def collect(merged, attn, inner, outer, vectors, widened):
    return (
        lax.all_gather(merged, ("dp", "fsdp"), axis=0, tiled=True),
        lax.all_gather(attn, ("dp", "fsdp"), axis=0, tiled=True),
        lax.all_gather(inner, ("dp", "fsdp"), axis=0, tiled=True),
        lax.all_gather(outer, ("dp", "fsdp"), axis=0, tiled=True),
        lax.all_gather(vectors, ("dp", "fsdp"), axis=0, tiled=True),
        lax.all_gather(widened, ("dp", "fsdp"), axis=0, tiled=True),
    )


def reduce_grads(merged, attn, inner, outer, vectors, widened):
    return (
        lax.psum_scatter(merged, ("dp", "fsdp"), scatter_dimension=0, tiled=True),
        lax.psum_scatter(attn, ("dp", "fsdp"), scatter_dimension=0, tiled=True),
        lax.psum_scatter(inner, ("dp", "fsdp"), scatter_dimension=0, tiled=True),
        lax.psum_scatter(outer, ("dp", "fsdp"), scatter_dimension=0, tiled=True),
        lax.psum_scatter(vectors, ("dp", "fsdp"), scatter_dimension=0, tiled=True),
        lax.psum_scatter(widened, ("dp", "fsdp"), scatter_dimension=0, tiled=True),
    )


def split_heads(projected, segments):
    total_rows, triple = projected.shape
    width = triple // 3
    return projected.reshape(segments, total_rows // segments, 3, HEADS, width // HEADS)


def attention_probs(queries, keysets, keep, scale):
    scores = (
        jnp.einsum("sqhd,skhd->shqk", queries, keysets, preferred_element_type=jnp.float32) * scale
    )
    scores = jnp.where(keep[:, None, None, :] > 0, scores, neg_fill)
    peaks = jnp.max(scores, axis=-1, keepdims=True)
    raised = jnp.exp(scores - peaks)
    return raised / jnp.sum(raised, axis=-1, keepdims=True)


def forward_pass(rows, keep, weights):
    merged, attn, inner, outer, vectors, widened = weights
    vector_full = vectors.astype(jnp.float32)
    width = rows.shape[1]
    scale = (width // HEADS) ** (-0.5)
    merged_bias = jnp.concatenate(
        (vector_full[:, 0], jnp.zeros((width,), jnp.float32), vector_full[:, 1])
    )
    projected = (jnp.dot(rows, merged, preferred_element_type=jnp.float32) + merged_bias).astype(
        jnp.bfloat16
    )
    split = split_heads(projected, keep.shape[0])
    probs = attention_probs(split[:, :, 0], split[:, :, 1], keep, scale).astype(jnp.bfloat16)
    context = jnp.einsum(
        "shqk,skhd->sqhd", probs, split[:, :, 2], preferred_element_type=jnp.float32
    )
    context = context.reshape(rows.shape[0], width).astype(jnp.bfloat16)
    attended = jnp.dot(context, attn, preferred_element_type=jnp.float32) + vector_full[:, 2]
    first_sum = rows.astype(jnp.float32) + attended
    first_norm = normalize(first_sum, vector_full[:, 3], vector_full[:, 4])
    first_low = first_norm.astype(jnp.bfloat16)
    inner_act = jnp.dot(first_low, inner, preferred_element_type=jnp.float32) + widened.astype(
        jnp.float32
    )
    activated = exact_gelu(inner_act).astype(jnp.bfloat16)
    outer_act = jnp.dot(activated, outer, preferred_element_type=jnp.float32) + vector_full[:, 5]
    second_sum = first_norm + outer_act
    encoded = normalize(second_sum, vector_full[:, 6], vector_full[:, 7]).astype(jnp.bfloat16)
    return (encoded, (projected, context, first_sum, first_low, inner_act, activated, second_sum))


def backward_pass(rows, keep, cotangent, weights, kept):
    merged, attn, inner, outer, vectors, widened = weights
    projected, context, first_sum, first_low, inner_act, activated, second_sum = kept
    vector_full = vectors.astype(jnp.float32)
    width = rows.shape[1]
    scale = (width // HEADS) ** (-0.5)
    second_out, second_pull = jax.vjp(normalize, second_sum, vector_full[:, 6], vector_full[:, 7])
    second_grad, second_gain_g, second_shift_g = second_pull(cotangent.astype(jnp.float32))
    outer_low = second_grad.astype(jnp.bfloat16)
    outer_bias_g = jnp.sum(outer_low.astype(jnp.float32), axis=0)
    outer_weight_g = contract_rows(activated, outer_low)
    act_grad = times_transposed(outer_low, outer)
    gelu_out, gelu_pull = jax.vjp(exact_gelu, inner_act)
    inner_low = gelu_pull(act_grad)[0].astype(jnp.bfloat16)
    inner_bias_g = jnp.sum(inner_low.astype(jnp.float32), axis=0)
    inner_weight_g = contract_rows(first_low, inner_low)
    first_total = second_grad + times_transposed(inner_low, inner)
    first_out, first_pull = jax.vjp(normalize, first_sum, vector_full[:, 3], vector_full[:, 4])
    first_grad, first_gain_g, first_shift_g = first_pull(first_total)
    attended_low = first_grad.astype(jnp.bfloat16)
    attn_bias_g = jnp.sum(attended_low.astype(jnp.float32), axis=0)
    attn_weight_g = contract_rows(context, attended_low)
    context_low = times_transposed(attended_low, attn).astype(jnp.bfloat16)
    split = split_heads(projected, keep.shape[0])
    queries = split[:, :, 0]
    keysets = split[:, :, 1]
    valuesets = split[:, :, 2]
    probs = attention_probs(queries, keysets, keep, scale)
    probs_low = probs.astype(jnp.bfloat16)
    context_heads = context_low.reshape(queries.shape)
    prob_grad = jnp.einsum(
        "sqhd,skhd->shqk", context_heads, valuesets, preferred_element_type=jnp.float32
    )
    value_grad = jnp.einsum(
        "shqk,sqhd->skhd", probs_low, context_heads, preferred_element_type=jnp.float32
    )
    score_low = (probs * (prob_grad - jnp.sum(probs * prob_grad, axis=-1, keepdims=True))).astype(
        jnp.bfloat16
    )
    query_grad = (
        jnp.einsum("shqk,skhd->sqhd", score_low, keysets, preferred_element_type=jnp.float32)
        * scale
    )
    key_grad = (
        jnp.einsum("shqk,sqhd->skhd", score_low, queries, preferred_element_type=jnp.float32)
        * scale
    )
    merged_low = jnp.stack((query_grad, key_grad, value_grad), axis=2).astype(jnp.bfloat16)
    merged_low = merged_low.reshape(rows.shape[0], 3 * width)
    merged_weight_g = contract_rows(rows, merged_low)
    merged_bias_g = jnp.sum(merged_low.astype(jnp.float32), axis=0)
    states_part = first_grad + times_transposed(merged_low, merged)
    vector_grads = jnp.stack(
        (
            merged_bias_g[:width],
            merged_bias_g[2 * width :],
            attn_bias_g,
            first_gain_g,
            first_shift_g,
            outer_bias_g,
            second_gain_g,
            second_shift_g,
        ),
        axis=1,
    )
    return (
        states_part,
        (
            merged_weight_g,
            attn_weight_g,
            inner_weight_g,
            outer_weight_g,
            vector_grads,
            inner_bias_g,
        ),
    )


def shards(
    states,
    pad_mask,
    query_proj,
    key_proj,
    value_proj,
    attn_proj,
    query_bias,
    value_bias,
    attn_bias,
    first_gain,
    first_shift,
    inner_proj,
    inner_bias,
    outer_proj,
    outer_bias,
    second_gain,
    second_shift,
    out_grad,
):
    width = states.shape[1]
    segments = pad_mask.shape[0] // MICRO
    block_rows = segments * pad_mask.shape[1]
    merged_shard = jnp.concatenate((query_proj, key_proj, value_proj), axis=1)
    vector_shard = jnp.stack(
        (
            query_bias,
            value_bias,
            attn_bias,
            first_gain,
            first_shift,
            outer_bias,
            second_gain,
            second_shift,
        ),
        axis=1,
    )
    fetched = collect(merged_shard, attn_proj, inner_proj, outer_proj, vector_shard, inner_bias)
    encoded_parts = []
    saved = []
    for index in range(MICRO):
        rows = lax.slice_in_dim(states, index * block_rows, (index + 1) * block_rows)
        keep = lax.slice_in_dim(pad_mask, index * segments, (index + 1) * segments)
        encoded, kept = forward_pass(rows, keep, fetched)
        encoded_parts.append(encoded)
        saved.append(kept)
    weights_back = collect(
        merged_shard, attn_proj, inner_proj, outer_proj, vector_shard, inner_bias
    )
    grad_parts = []
    totals = None
    for index in range(MICRO):
        rows = lax.slice_in_dim(states, index * block_rows, (index + 1) * block_rows)
        keep = lax.slice_in_dim(pad_mask, index * segments, (index + 1) * segments)
        cotangent = lax.slice_in_dim(out_grad, index * block_rows, (index + 1) * block_rows)
        states_part, pieces = backward_pass(rows, keep, cotangent, weights_back, saved[index])
        grad_parts.append(states_part)
        totals = pieces if index == 0 else jax.tree.map(jnp.add, totals, pieces)
    summed = reduce_grads(totals[0], totals[1], totals[2], totals[3], totals[4], totals[5])
    merged_sum, attn_sum, inner_sum, outer_sum, vector_sum, widened_sum = summed
    return (
        jnp.concatenate(encoded_parts, axis=0),
        jnp.concatenate(grad_parts, axis=0),
        merged_sum[:, :width],
        merged_sum[:, width : 2 * width],
        merged_sum[:, 2 * width :],
        attn_sum,
        vector_sum[:, 0],
        vector_sum[:, 1],
        vector_sum[:, 2],
        vector_sum[:, 3],
        vector_sum[:, 4],
        inner_sum,
        widened_sum,
        outer_sum,
        vector_sum[:, 5],
        vector_sum[:, 6],
        vector_sum[:, 7],
    )


def solution(mesh):
    return jax.shard_map(
        shards,
        mesh=mesh,
        in_specs=(
            P(("dp", "fsdp"), None),
            P(("dp", "fsdp"), None),
            P(("dp", "fsdp"), None),
            P(("dp", "fsdp"), None),
            P(("dp", "fsdp"), None),
            P(("dp", "fsdp"), None),
            P(("dp", "fsdp")),
            P(("dp", "fsdp")),
            P(("dp", "fsdp")),
            P(("dp", "fsdp")),
            P(("dp", "fsdp")),
            P(("dp", "fsdp"), None),
            P(("dp", "fsdp")),
            P(("dp", "fsdp"), None),
            P(("dp", "fsdp")),
            P(("dp", "fsdp")),
            P(("dp", "fsdp")),
            P(("dp", "fsdp"), None),
        ),
        out_specs=(
            P(("dp", "fsdp"), None),
            P(("dp", "fsdp"), None),
            P(("dp", "fsdp"), None),
            P(("dp", "fsdp"), None),
            P(("dp", "fsdp"), None),
            P(("dp", "fsdp"), None),
            P(("dp", "fsdp")),
            P(("dp", "fsdp")),
            P(("dp", "fsdp")),
            P(("dp", "fsdp")),
            P(("dp", "fsdp")),
            P(("dp", "fsdp"), None),
            P(("dp", "fsdp")),
            P(("dp", "fsdp"), None),
            P(("dp", "fsdp")),
            P(("dp", "fsdp")),
            P(("dp", "fsdp")),
        ),
        check_vma=False,
    )
```

profile of v0, /device:TPU:0, one launch (start us, length us, event | category | flops | bytes accessed | tf_op | source)
XLA Modules:
  0.0 1225.5 jit_solution(250411452194497344)
XLA Ops:
  11.8 43.8 %all-gather = bf16[32,32,8]{1,2,0:T(8,128)(2,1)S(1)} all-gather(bf16[1,32,8]{1,2,0:T(8,128)(2,1)S(1)} %bitcast.264), channel_id=1, replica_groups=mesh['dp'=4,'fsdp'=8] {'dp','fsdp'}, dimensions={0}, use_global_device_ids=true | all-gather | bytes 16896 | tf_op jit(solution)/shard_map/all_gather | solution.py:42
  55.6 37.0 %all-gather.1 = bf16[32,1,128]{2,1,0:T(2,128)(2,1)S(1)} all-gather(bf16[1,1,128]{2,1,0:T(2,128)(2,1)} %bitcast.279), channel_id=1, replica_groups=mesh['dp'=4,'fsdp'=8] {'dp','fsdp'}, dimensions={0}, use_global_device_ids=true | all-gather | bytes 8448 | tf_op jit(solution)/shard_map/all_gather | solution.py:43
  94.6 5.0 fusion.16
  107.9 6.3 fusion.17
  118.8 3.5 fusion.113
  124.9 17.0 %all-gather.9.cloned.1.call-done = bf16[1024,1024]{1,0:T(8,128)(2,1)} async-done(((bf16[32,1024]{1,0:T(8,128)(2,1)}), bf16[1024,1024]{1,0:T(8,128)(2,1)}) %all-gather.9.cloned.1.call-update) | async-done | bytes 2097168 | tf_op jit(solution)/shard_map/all_gather | solution.py:39
  147.0 74.3 %all-gather.11.cloned.1.call-done = bf16[1024,4096]{1,0:T(8,128)(2,1)} async-done(((bf16[32,4096]{1,0:T(8,128)(2,1)}), bf16[1024,4096]{1,0:T(8,128)(2,1)}) %all-gather.11.cloned.1.call-update) | async-done | bytes 8388624 | tf_op jit(solution)/shard_map/all_gather | solution.py:40
  221.3 16.2 %multiply_convert_fusion = (bf16[256,4096]{1,0:T(8,128)(2,1)}, f32[256,4096]{1,0:T(8,128)}, f32[256,4096]{1,0:T(8,128)}) fusion(f32[4096]{0:T(1024)S(1)} %bitcast.260, bf16[1024,4096]{1,0:T(8,128)(2,1)} %all-gather.11.cloned.1.call-done, f32[256,1024]{1,0:T(8,128)S(1)} %get-tuple-element.158, f32[256]{0:T(256)S(1)} %fusion.86, ...), kind=kOutput, calls=%fused_computation.15 | convolution fusion | flops 2218000384 | bytes 19949568 | tf_op jit(solution)/shard_map/dot_general | solution.py:95
  237.5 62.6 %all-gather.13.cloned.1.call-done = bf16[4096,1024]{1,0:T(8,128)(2,1)} async-done(((bf16[128,1024]{1,0:T(8,128)(2,1)}), bf16[4096,1024]{1,0:T(8,128)(2,1)}) %all-gather.13.cloned.1.call-update) | async-done | bytes 8388624 | tf_op jit(solution)/shard_map/all_gather | solution.py:41
  300.1 6.6 fusion.112
  307.1 16.7 %multiply_convert_fusion.1 = (bf16[256,4096]{1,0:T(8,128)(2,1)S(1)}, f32[256,4096]{1,0:T(8,128)}, f32[256,4096]{1,0:T(8,128)}) fusion(f32[4096]{0:T(1024)S(1)} %bitcast.261, bf16[1024,4096]{1,0:T(8,128)(2,1)S(1)} %copy-done.58, f32[256,1024]{1,0:T(8,128)S(1)} %get-tuple-element.165, f32[1024]{0:T(1024)S(1)} %bitcast.243, f32[1024]{0:T(1024)S(1)} %bitcast.235, ...), kind=kOutput, calls=%fused_computation.28 | convolution fusion | flops 2218000384 | bytes 19949568 | tf_op jit(solution)/shard_map/dot_general | solution.py:95
  330.1 11.6 convert_reduce_fusion
  341.8 6.8 convolution_add_fusion.9
  348.6 11.8 convert_reduce_fusion.1
  360.5 7.2 multiply_reduce_fusion.3
  375.8 3.4 convolution_bitcast_fusion
  396.2 2.8 copy.108
  401.2 6.4 fusion.23
  409.1 11.6 add_bitcast_fusion
  420.7 12.6 %copy.120 = f32[1024,3072]{1,0:T(8,128)} copy(f32[1024,3072]{0,1:T(8,128)} %add_bitcast_fusion) | data formatting | bytes 25165824
  439.0 4.1 fusion.94
  443.1 9.9 convolution_add_fusion.1
  454.1 4.0 fusion.116
  458.1 9.2 convolution_add_fusion
  468.1 39.5 %all-reduce = f32[4096]{0:T(1024)S(1)} all-reduce(f32[4096]{0:T(1024)S(1)} %add.234), channel_id=6, replica_groups=mesh['dp'=4,'fsdp'=8] {'dp','fsdp'}, use_global_device_ids=true, to_apply=%region_42.43.clone | all-reduce | flops 4096 | bytes 32768
  510.3 4.8 fusion.40
  515.1 4.7 fusion.37
  521.3 20.6 %reduce-scatter.18.cloned.1.call-done = f32[32,8]{1,0:T(8,128)} async-done(((f32[1024,8]{1,0:T(8,128)}), f32[32,8]{1,0:T(8,128)}) %reduce-scatter.18.cloned.1.call-update) | async-done | bytes 1040
  547.6 152.8 %reduce-scatter.16.cloned.1.call-done = f32[32,3072]{1,0:T(8,128)} async-done(((f32[1024,3072]{1,0:T(8,128)}), f32[32,3072]{1,0:T(8,128)}) %reduce-scatter.16.cloned.1.call-update) | async-done | bytes 393232
  702.2 142.9 %reduce-scatter.10.cloned.1.call-done = f32[32,1024]{1,0:T(8,128)} async-done(((f32[1024,1024]{1,0:T(8,128)}), f32[32,1024]{1,0:T(8,128)}) %reduce-scatter.10.cloned.1.call-update) | async-done | bytes 131088 | tf_op jit(solution)/shard_map/reduce_scatter | solution.py:50
  845.1 186.4 %reduce-scatter.12.cloned.1.call-done = f32[32,4096]{1,0:T(8,128)} async-done(((f32[1024,4096]{1,0:T(8,128)}), f32[32,4096]{1,0:T(8,128)}) %reduce-scatter.12.cloned.1.call-update) | async-done | bytes 524304 | tf_op jit(solution)/shard_map/reduce_scatter | solution.py:51
  1031.5 187.3 %reduce-scatter.14.cloned.1.call-done = f32[128,1024]{1,0:T(8,128)} async-done(((f32[4096,1024]{1,0:T(8,128)}), f32[128,1024]{1,0:T(8,128)}) %reduce-scatter.14.cloned.1.call-update) | async-done | bytes 524304 | tf_op jit(solution)/shard_map/reduce_scatter | solution.py:52
  (237 shorter events, 81.1 us)
Async XLA Ops:
  7.2 87.4 %all-gather.7.cloned.1.call-start = ((), (), s32[]{:S(2)}) async-start(), calls=%async_computation.5 | async-start | bytes 6488064 | tf_op jit(solution)/shard_map/all_gather | solution.py:38
  8.9 133.1 %all-gather.9.cloned.1.call-start = ((), (), s32[]{:S(2)}) async-start(), calls=%async_computation.6 | async-start | bytes 2162688 | tf_op jit(solution)/shard_map/all_gather | solution.py:39
  9.6 211.6 %all-gather.11.cloned.1.call-start = ((), (), s32[]{:S(2)}) async-start(), calls=%async_computation.7 | async-start | bytes 8650752 | tf_op jit(solution)/shard_map/all_gather | solution.py:40
  10.3 289.8 %all-gather.13.cloned.1.call-start = ((), (), s32[]{:S(2)}) async-start(), calls=%async_computation.8 | async-start | bytes 8650752 | tf_op jit(solution)/shard_map/all_gather | solution.py:41
  10.9 530.9 %reduce-scatter.18.cloned.1.call-start = ((), (), s32[]{:S(2)}) async-start(), calls=%async_computation.13 | async-start | bytes 540672
  107.9 34.1 %copy-start.7 = (bf16[2,128,16,64]{1,0,3,2:T(2,128)(2,1)}, bf16[2,128,16,64]{1,0,3,2:T(2,128)(2,1)S(1)}, u32[]{:S(2)}) copy-start(bf16[2,128,16,64]{1,0,3,2:T(2,128)(2,1)S(1)} %copy.94) | copy-start | bytes 1572868
  124.9 21.7 %copy-start.9 = (bf16[2,128,16,64]{1,0,3,2:T(2,128)(2,1)}, bf16[2,128,16,64]{1,0,3,2:T(2,128)(2,1)S(1)}, u32[]{:S(2)}) copy-start(bf16[2,128,16,64]{1,0,3,2:T(2,128)(2,1)S(1)} %copy.89) | copy-start | bytes 1572868
  144.5 76.7 %copy-start.48 = (f32[32,1,128]{2,1,0:T(1,128)S(1)}, f32[32,1,128]{2,1,0:T(1,128)}, u32[]{:S(2)}) copy-start(f32[32,1,128]{2,1,0:T(1,128)} %convert_element_type.197) | copy-start | bytes 49156
  147.0 220.7 %copy-start.49 = (f32[256]{0:T(256)}, f32[256]{0:T(256)S(1)}, u32[]{:S(2)}) copy-start(f32[256]{0:T(256)S(1)} %fusion.86) | copy-start | bytes 3076
  221.3 78.9 %copy-start.53 = (f32[1024,1]{0,1:T(1,128)S(1)}, f32[1024,1]{0,1:T(1,128)}, u32[]{:S(2)}) copy-start(f32[1024,1]{0,1:T(1,128)} %get-tuple-element.130) | copy-start | bytes 12292
  300.1 6.9 copy-start.58
  300.1 23.6 %slice-start = ((s8[8388608]{0:T(1024)(128)(4,1)}), s8[4194304]{0:T(1024)(128)(4,1)S(1)}, s32[]{:S(2)}) async-start(s8[8388608]{0:T(1024)(128)(4,1)} %bitcast.288), calls=%async_computation.14 | async-start | bytes 8388608
  307.1 16.7 %slice-start.1 = ((s8[8388608]{0:T(1024)(128)(4,1)}), s8[4194304]{0:T(1024)(128)(4,1)S(1)}, s32[]{:S(2)}) async-start(s8[8388608]{0:T(1024)(128)(4,1)} %bitcast.288), calls=%async_computation.15 | async-start | bytes 8388608
  329.6 12.1 copy-start.36
  329.8 18.8 %copy-start.24 = (bf16[256,1024]{1,0:T(8,128)(2,1)}, bf16[256,1024]{1,0:T(8,128)(2,1)S(1)}, u32[]{:S(2)}) copy-start(bf16[256,1024]{1,0:T(8,128)(2,1)S(1)} %get-tuple-element.97) | copy-start | bytes 1572868
  341.8 6.8 copy-start.19
  341.8 6.8 copy-start.60
  360.5 7.2 copy-start.35
  369.3 6.4 copy-start.44
  369.3 9.8 copy-start.54
  373.7 5.5 copy-start.40
  382.0 8.0 copy-start.43
  382.0 10.8 copy-start.56
  401.2 6.4 copy-start.4
  409.1 291.4 %reduce-scatter.16.cloned.1.call-start = ((), (), s32[]{:S(2)}) async-start(), calls=%async_computation.12 | async-start | bytes 12976128
  433.4 411.8 %reduce-scatter.10.cloned.1.call-start = ((), (), s32[]{:S(2)}) async-start(), calls=%async_computation.9 | async-start | bytes 4325376 | tf_op jit(solution)/shard_map/reduce_scatter | solution.py:50
  438.9 592.5 %reduce-scatter.12.cloned.1.call-start = ((), (), s32[]{:S(2)}) async-start(), calls=%async_computation.10 | async-start | bytes 17301504 | tf_op jit(solution)/shard_map/reduce_scatter | solution.py:51
  453.1 765.6 %reduce-scatter.14.cloned.1.call-start = ((), (), s32[]{:S(2)}) async-start(), calls=%async_computation.11 | async-start | bytes 17301504 | tf_op jit(solution)/shard_map/reduce_scatter | solution.py:52
  467.3 40.8 %copy-start.23 = (bf16[256,1024]{1,0:T(8,128)(2,1)S(1)}, bf16[256,1024]{1,0:T(8,128)(2,1)}, u32[]{:S(2)}) copy-start(bf16[256,1024]{1,0:T(8,128)(2,1)} %get-tuple-element.121) | copy-start | bytes 1572868
  467.3 42.9 %copy-start = (bf16[2,128,3,16,64]{1,0,4,3,2:T(2,128)(2,1)S(1)}, bf16[2,128,3,16,64]{1,0,4,3,2:T(2,128)(2,1)}, u32[]{:S(2)}) copy-start(bf16[2,128,3,16,64]{1,0,4,3,2:T(2,128)(2,1)} %copy.108) | copy-start | bytes 4718596
  467.3 42.9 %copy-start.16 = (f32[256,1024]{1,0:T(8,128)S(1)}, f32[256,1024]{1,0:T(8,128)}, u32[]{:S(2)}) copy-start(f32[256,1024]{1,0:T(8,128)} %copy-done.15) | copy-start | bytes 3145732
  467.3 42.9 %copy-start.55 = (f32[256]{0:T(256)S(1)}, f32[256]{0:T(256)}, u32[]{:S(2)}) copy-start(f32[256]{0:T(256)} %copy-done.54) | copy-start | bytes 3076
  (40 other events, 95.2 us)
Sparse Core Ops, SparseCore 0:
  11.6 72.3 all-gather.6
  86.9 54.9 all-gather.8
  145.0 76.2 all-gather.10
  224.1 75.9 all-gather.12
  409.2 132.5 reduce-scatter.17
  548.7 151.6 reduce-scatter.15
  703.3 141.7 reduce-scatter.9
  848.0 183.4 reduce-scatter.11
  1034.3 184.3 reduce-scatter.13
where the time goes:
time: 1230 us
  waiting for transfers between devices  846 us (69%)
  matrix products  175 us (14%)
  blocking collectives  120 us (10%)
  local copies, waits for them, and re-layouts  53.7 us (4%)
  between operations  15 us (1%)
  other arithmetic  14.8 us (1%)
    reduce_scatter x1, waiting for transfers between devices, reduce_grads(): lax.psum_scatter(outer, ('dp', 'fsdp'), scatter_dimension=0, tiled=True)  187 us
    reduce_scatter x1, waiting for transfers between devices, reduce_grads(): lax.psum_scatter(inner, ('dp', 'fsdp'), scatter_dimension=0, tiled=True)  186 us
    unnamed x11, waiting for transfers between devices  175 us
    reduce_scatter x1, waiting for transfers between devices, reduce_grads(): lax.psum_scatter(attn, ('dp', 'fsdp'), scatter_dimension=0, tiled=True)  143 us
    all_gather x1, waiting for transfers between devices, collect(): lax.all_gather(inner, ('dp', 'fsdp'), axis=0, tiled=True)  74.3 us
    all_gather x1, waiting for transfers between devices, collect(): lax.all_gather(outer, ('dp', 'fsdp'), axis=0, tiled=True)  62.6 us
    dot_general x8, matrix products, contract_rows(): lax.dot_general(left, right, (((0,), (0,)), ((), ())), preferred_element_...  49.8 us
    dot_general x8, matrix products, times_transposed(): lax.dot_general(left, right, (((1,), (1,)), ((), ())), preferred_element_...  49.2 us
  transfers between devices with their start and end apart: 9, of which 8 were waited for; matrix products, arithmetic and copies ran while one was open for 11% of the time, Pallas kernels for 0%

commit v1 on v0

--- a/solution.py
+++ b/solution.py
@@ -1,14 +1,358 @@
+import functools
+
 import jax
 import jax.numpy as jnp
 from jax import lax
+from jax.experimental import pallas as pl
+from jax.experimental.pallas import tpu as pltpu
 from jax.sharding import PartitionSpec as P
 
 HEADS = 16
-MICRO = 2
-
+MESH = pl.DeviceIdType.MESH
 
 epsilon = 1e-05
 neg_fill = -1e30
+
+
+class Place:
+    def __init__(self, depth):
+        dp = lax.axis_index("dp")
+        fsdp = lax.axis_index("fsdp")
+        self.depth = depth
+        self.dp = dp
+        self.z = fsdp // 2
+        self.core = lax.rem(fsdp, 2)
+        flip_x = dp + 1 - 2 * lax.rem(dp, 2)
+        flip_y = lax.rem(dp + 2, 4)
+        self.near = flip_x + self.core * (flip_y - flip_x)
+        self.far = flip_y + self.core * (flip_x - flip_y)
+        self.both = lax.rem(flip_x + 2, 4)
+        self.fsdp = fsdp
+        self.sibling = fsdp + 1 - 2 * self.core
+
+    def up(self, step):
+        return lax.rem(self.z + step, self.depth)
+
+    def down(self, step):
+        return lax.rem(self.z + self.depth - step, self.depth)
+
+    def along(self, z):
+        return (self.dp, z * 2 + self.core)
+
+    def greet(self):
+        barrier = pltpu.get_barrier_semaphore()
+        others = [self.along(self.up(step)) for step in range(1, self.depth)]
+        others += [(self.near, self.fsdp), (self.far, self.fsdp), (self.dp, self.sibling)]
+        for other in others:
+            pl.semaphore_signal(barrier, inc=1, device_id=other, device_id_type=MESH)
+        pl.semaphore_wait(barrier, len(others))
+
+
+def remote(source, target, send, recv, device):
+    return pltpu.make_async_remote_copy(
+        src_ref=source, dst_ref=target, send_sem=send, recv_sem=recv, device_id=device, device_id_type=MESH
+    )
+
+
+class Gather:
+    def __init__(self, place, full, sems, piece):
+        self.place, self.full, self.piece = place, full, piece
+        self.sz, self.rz, self.sb, self.rb, self.sa, self.ra, self.sc, self.rc = sems
+
+    def copy_z(self, step, arriving=False):
+        p = self.place
+        z = p.down(step) if arriving else p.z
+        block = self.full.at[p.dp, z, p.core]
+        return remote(block, block, self.sz.at[self.piece, step - 1], self.rz.at[self.piece, step - 1], p.along(p.up(step)))
+
+    def copy_near(self, step, arriving=False):
+        p = self.place
+        block = self.full.at[p.near if arriving else p.dp, p.down(step), p.core]
+        return remote(block, block, self.sb.at[self.piece, step], self.rb.at[self.piece, step], (p.near, p.fsdp))
+
+    def copy_far(self, half, step, arriving=False):
+        p = self.place
+        row = (p.both if half else p.far) if arriving else (p.near if half else p.dp)
+        block = self.full.at[row, p.down(step), p.core]
+        at = half * p.depth + step
+        return remote(block, block, self.sa.at[self.piece, at], self.ra.at[self.piece, at], (p.far, p.fsdp))
+
+    def copy_core(self, part, arriving=False):
+        p = self.place
+        if arriving:
+            row = (p.dp, p.far, p.near, p.both)[part]
+            block = self.full.at[row, :, 1 - p.core]
+        else:
+            row = (p.dp, p.near, p.far, p.both)[part]
+            block = self.full.at[row, :, p.core]
+        return remote(block, block, self.sc.at[self.piece, part], self.rc.at[self.piece, part], (p.dp, p.sibling))
+
+    def start_z(self):
+        for step in range(1, self.place.depth):
+            self.copy_z(step).start()
+        self.copy_near(0).start()
+        self.copy_far(0, 0).start()
+
+    def spread(self):
+        for step in range(1, self.place.depth):
+            self.copy_z(step, True).wait_recv()
+            self.copy_near(step).start()
+            self.copy_far(0, step).start()
+        self.copy_core(0).start()
+
+    def spread_far(self):
+        for step in range(self.place.depth):
+            self.copy_near(step, True).wait_recv()
+            self.copy_far(1, step).start()
+        self.copy_core(1).start()
+
+    def finish(self):
+        p = self.place
+        for half in range(2):
+            for step in range(p.depth):
+                self.copy_far(half, step, True).wait_recv()
+            self.copy_core(2 + half).start()
+        for part in range(4):
+            self.copy_core(part, True).wait_recv()
+
+    def drain(self):
+        p = self.place
+        for step in range(1, p.depth):
+            self.copy_z(step).wait_send()
+        for step in range(p.depth):
+            self.copy_near(step).wait_send()
+            self.copy_far(0, step).wait_send()
+            self.copy_far(1, step).wait_send()
+        for part in range(4):
+            self.copy_core(part).wait_send()
+
+
+def gather_sems(pieces, depth):
+    counts = (depth - 1, depth - 1, depth, depth, 2 * depth, 2 * depth, 4, 4)
+    return [pltpu.SemaphoreType.DMA((pieces, count)) for count in counts]
+
+
+def gather_kernel(depth, groups, *refs):
+    count = sum(groups)
+    sources = refs[:count]
+    fulls = refs[count : count + len(groups)]
+    own_sem = refs[count + len(groups)]
+    sems = refs[count + len(groups) + 1 :]
+    place = Place(depth)
+    local = []
+    at = 0
+    for full, parts in zip(fulls, groups):
+        width = full.shape[4] // parts
+        for part in range(parts):
+            target = full.at[place.dp, place.z, place.core, :, pl.ds(part * width, width)]
+            local.append(pltpu.make_async_copy(sources[at], target, own_sem.at[at]))
+            at += 1
+    for copy in local:
+        copy.start()
+    place.greet()
+    for copy in local:
+        copy.wait()
+    nets = [Gather(place, full, sems, piece) for piece, full in enumerate(fulls)]
+    for net in nets:
+        net.start_z()
+    for net in nets:
+        net.spread()
+        net.spread_far()
+    for net in nets:
+        net.finish()
+    for net in nets:
+        net.drain()
+
+
+def gather_all(depth, groups):
+    flat = [block for group in groups for block in group]
+    shapes = []
+    for group in groups:
+        rows = group[0].shape[0]
+        columns = sum(block.shape[1] for block in group)
+        shapes.append(jax.ShapeDtypeStruct((4, depth, 2, rows, columns), group[0].dtype))
+    return pl.pallas_call(
+        functools.partial(gather_kernel, depth, tuple(len(group) for group in groups)),
+        out_shape=shapes,
+        in_specs=[pl.BlockSpec(memory_space=pl.ANY)] * len(flat),
+        out_specs=[pl.BlockSpec(memory_space=pl.ANY)] * len(shapes),
+        scratch_shapes=[pltpu.SemaphoreType.DMA((len(flat),))] + gather_sems(len(groups), depth),
+        compiler_params=pltpu.CompilerParams(collective_id=0, has_side_effects=True),
+        name="gather_weights",
+    )(*flat)
+
+
+def add_into(target, other):
+    count, rows, _ = target.shape
+    tile = 8 if target.dtype == jnp.float32 else 16
+    steps = rows // tile
+
+    def one(index, _):
+        part = index // steps
+        at = pl.ds(pl.multiple_of(lax.rem(index, steps) * tile, tile), tile)
+        target[part, at, :] = target[part, at, :] + other[part, at, :]
+        return 0
+
+    lax.fori_loop(0, count * steps, one, 0)
+
+
+class Scatter:
+    def __init__(self, place, sums, slots, sems, piece):
+        self.place, self.sums, self.piece = place, sums, piece
+        self.from_core, self.from_far, self.from_near, self.from_z = slots
+        self.sc, self.rc, self.sa, self.ra, self.sb, self.rb, self.sz, self.rz = sems
+
+    def copy_core(self, whole, part):
+        p = self.place
+        return remote(
+            whole.at[part, :, 1 - p.core], self.from_core.at[part], self.sc.at[self.piece, part],
+            self.rc.at[self.piece, part], (p.dp, p.sibling),
+        )
+
+    def rows_of(self, half, away):
+        p = self.place
+        if away:
+            return p.both if half else p.far
+        return p.near if half else p.dp
+
+    def copy_far(self, half):
+        p = self.place
+        return remote(
+            self.sums.at[self.rows_of(half, True)], self.from_far.at[half], self.sa.at[self.piece, half],
+            self.ra.at[self.piece, half], (p.far, p.fsdp),
+        )
+
+    def copy_near(self):
+        p = self.place
+        return remote(
+            self.sums.at[p.near], self.from_near, self.sb.at[self.piece], self.rb.at[self.piece], (p.near, p.fsdp)
+        )
+
+    def copy_z(self, step):
+        p = self.place
+        return remote(
+            self.sums.at[p.dp, p.up(step)], self.from_z.at[step - 1], self.sz.at[self.piece, step - 1],
+            self.rz.at[self.piece, step - 1], p.along(p.up(step)),
+        )
+
+    def add_core(self, whole):
+        p = self.place
+        for half in (1, 0):
+            for away in (True, False):
+                row = self.rows_of(half, away)
+                self.copy_core(whole, row).wait_recv()
+                add_into(self.sums.at[row], self.from_core.at[row])
+                if away:
+                    self.copy_far(half).start()
+
+    def add_far(self, half):
+        self.copy_far(half).wait_recv()
+        add_into(self.sums.at[self.rows_of(half, False)], self.from_far.at[half])
+        if half:
+            self.copy_near().start()
+
+    def add_near(self):
+        p = self.place
+        self.copy_near().wait_recv()
+        add_into(self.sums.at[p.dp], self.from_near)
+        for step in range(1, p.depth):
+            self.copy_z(step).start()
+
+    def finish(self, out):
+        p = self.place
+        for step in range(1, p.depth):
+            self.copy_z(step).wait_recv()
+        rows = out.shape[0]
+        tile = 8 if self.sums.dtype == jnp.float32 else 16
+
+        def one(index, _):
+            at = pl.ds(pl.multiple_of(index * tile, tile), tile)
+            total = self.sums[p.dp, p.z, at, :].astype(jnp.float32)
+            for step in range(p.depth - 1):
+                total = total + self.from_z[step, at, :].astype(jnp.float32)
+            out[at, :] = total
+            return 0
+
+        lax.fori_loop(0, rows // tile, one, 0)
+
+    def drain(self, whole):
+        for part in range(4):
+            self.copy_core(whole, part).wait_send()
+        self.copy_far(1).wait_send()
+        self.copy_far(0).wait_send()
+        self.copy_near().wait_send()
+        for step in range(1, self.place.depth):
+            self.copy_z(step).wait_send()
+
+
+def scatter_sems(pieces, depth):
+    dma = pltpu.SemaphoreType.DMA
+    return [
+        dma((pieces, 4)), dma((pieces, 4)), dma((pieces, 2)), dma((pieces, 2)), dma((pieces,)), dma((pieces,)),
+        dma((pieces, depth - 1)), dma((pieces, depth - 1)),
+    ]
+
+
+def scatter_slots(shape, dtype):
+    dps, depth, _, rows, columns = shape
+    return [
+        pltpu.VMEM((dps, depth, rows, columns), dtype),
+        pltpu.VMEM((dps, depth, rows, columns), dtype),
+        pltpu.VMEM((2, depth, rows, columns), dtype),
+        pltpu.VMEM((depth, rows, columns), dtype),
+        pltpu.VMEM((depth - 1, rows, columns), dtype),
+    ]
+
+
+def scatter_kernel(depth, count, *refs):
+    wholes = refs[:count]
+    outs = refs[count : 2 * count]
+    scratch = refs[2 * count : 7 * count]
+    own_sem = refs[7 * count]
+    sems = refs[7 * count + 1 :]
+    place = Place(depth)
+    nets = []
+    local = []
+    for piece in range(count):
+        sums, *slots = scratch[5 * piece : 5 * piece + 5]
+        nets.append(Scatter(place, sums, slots, sems, piece))
+        local.append(pltpu.make_async_copy(wholes[piece].at[:, :, place.core], sums, own_sem.at[piece]))
+    for copy in local:
+        copy.start()
+    place.greet()
+    for net, whole in zip(nets, wholes):
+        for half in (1, 0):
+            for away in (False, True):
+                net.copy_core(whole, net.rows_of(half, away)).start()
+    for piece in range(count):
+        local[piece].wait()
+        nets[piece].add_core(wholes[piece])
+    for net in nets:
+        net.add_far(1)
+        net.add_far(0)
+        net.add_near()
+    for net, out in zip(nets, outs):
+        net.finish(out)
+    for net, whole in zip(nets, wholes):
+        net.drain(whole)
+
+
+def scatter_all(depth, wholes):
+    shapes = [jax.ShapeDtypeStruct(whole.shape[3:], jnp.float32) for whole in wholes]
+    scratch = []
+    for whole in wholes:
+        scratch += scatter_slots(whole.shape, whole.dtype)
+    return pl.pallas_call(
+        functools.partial(scatter_kernel, depth, len(wholes)),
+        out_shape=shapes,
+        in_specs=[pl.BlockSpec(memory_space=pl.ANY)] * len(wholes),
+        out_specs=[pl.BlockSpec(memory_space=pltpu.VMEM)] * len(wholes),
+        scratch_shapes=scratch + [pltpu.SemaphoreType.DMA((len(wholes),))] + scatter_sems(len(wholes), depth),
+        compiler_params=pltpu.CompilerParams(
+            collective_id=1, has_side_effects=True, vmem_limit_bytes=60 * 1024 * 1024
+        ),
+        name="scatter_gradients",
+    )(*wholes)
 
 
 def normalize(hidden, gain, shift):
@@ -180,129 +524,82 @@
     )
 
 
-def shards(
-    states,
-    pad_mask,
-    query_proj,
-    key_proj,
-    value_proj,
-    attn_proj,
-    query_bias,
-    value_bias,
-    attn_bias,
-    first_gain,
-    first_shift,
-    inner_proj,
-    inner_bias,
-    outer_proj,
-    outer_bias,
-    second_gain,
-    second_shift,
-    out_grad,
-):
+def pack_vectors(vectors, widened):
+    flat = jnp.concatenate(list(vectors) + [widened])
+    rows = flat.shape[0] // 128
+    return jnp.pad(flat.reshape(rows, 128), ((0, 16 - rows), (0, 0)))
+
+
+def shards(depth, *arrays):
+    (states, pad_mask, query_proj, key_proj, value_proj, attn_proj, query_bias, value_bias, attn_bias, first_gain,
+     first_shift, inner_proj, inner_bias, outer_proj, outer_bias, second_gain, second_shift, out_grad) = arrays
     width = states.shape[1]
-    segments = pad_mask.shape[0] // MICRO
-    block_rows = segments * pad_mask.shape[1]
+    short = (query_bias, value_bias, attn_bias, first_gain, first_shift, outer_bias, second_gain, second_shift)
+    if depth:
+        return kernel_shards(depth, short, states, pad_mask, query_proj, key_proj, value_proj, attn_proj, inner_proj,
+                             inner_bias, outer_proj, out_grad)
     merged_shard = jnp.concatenate((query_proj, key_proj, value_proj), axis=1)
-    vector_shard = jnp.stack(
-        (
-            query_bias,
-            value_bias,
-            attn_bias,
-            first_gain,
-            first_shift,
-            outer_bias,
-            second_gain,
-            second_shift,
-        ),
-        axis=1,
-    )
-    fetched = collect(merged_shard, attn_proj, inner_proj, outer_proj, vector_shard, inner_bias)
-    encoded_parts = []
-    saved = []
-    for index in range(MICRO):
-        rows = lax.slice_in_dim(states, index * block_rows, (index + 1) * block_rows)
-        keep = lax.slice_in_dim(pad_mask, index * segments, (index + 1) * segments)
-        encoded, kept = forward_pass(rows, keep, fetched)
-        encoded_parts.append(encoded)
-        saved.append(kept)
-    weights_back = collect(
-        merged_shard, attn_proj, inner_proj, outer_proj, vector_shard, inner_bias
-    )
-    grad_parts = []
-    totals = None
-    for index in range(MICRO):
-        rows = lax.slice_in_dim(states, index * block_rows, (index + 1) * block_rows)
-        keep = lax.slice_in_dim(pad_mask, index * segments, (index + 1) * segments)
-        cotangent = lax.slice_in_dim(out_grad, index * block_rows, (index + 1) * block_rows)
-        states_part, pieces = backward_pass(rows, keep, cotangent, weights_back, saved[index])
-        grad_parts.append(states_part)
-        totals = pieces if index == 0 else jax.tree.map(jnp.add, totals, pieces)
-    summed = reduce_grads(totals[0], totals[1], totals[2], totals[3], totals[4], totals[5])
-    merged_sum, attn_sum, inner_sum, outer_sum, vector_sum, widened_sum = summed
-    return (
-        jnp.concatenate(encoded_parts, axis=0),
-        jnp.concatenate(grad_parts, axis=0),
-        merged_sum[:, :width],
-        merged_sum[:, width : 2 * width],
-        merged_sum[:, 2 * width :],
-        attn_sum,
-        vector_sum[:, 0],
-        vector_sum[:, 1],
-        vector_sum[:, 2],
-        vector_sum[:, 3],
-        vector_sum[:, 4],
-        inner_sum,
-        widened_sum,
-        outer_sum,
-        vector_sum[:, 5],
-        vector_sum[:, 6],
-        vector_sum[:, 7],
-    )
+    fetched = collect(merged_shard, attn_proj, inner_proj, outer_proj, jnp.stack(short, axis=1), inner_bias)
+    encoded, kept = forward_pass(states, pad_mask, fetched)
+    states_part, totals = backward_pass(states, pad_mask, out_grad, fetched, kept)
+    merged_sum, attn_sum, inner_sum, outer_sum, vector_sum, widened_sum = reduce_grads(*totals)
+    return ordered(encoded, states_part, merged_sum, attn_sum, inner_sum, outer_sum, vector_sum.T, widened_sum)
+
+
+def ordered(encoded, states_part, merged_sum, attn_sum, inner_sum, outer_sum, vectors, widened_sum):
+    width = attn_sum.shape[1]
+    return (encoded, states_part, merged_sum[:, :width], merged_sum[:, width : 2 * width], merged_sum[:, 2 * width :],
+            attn_sum, vectors[0], vectors[1], vectors[2], vectors[3], vectors[4], inner_sum, widened_sum, outer_sum,
+            vectors[5], vectors[6], vectors[7])
+
+
+def kernel_shards(depth, short, states, pad_mask, query_proj, key_proj, value_proj, attn_proj, inner_proj, inner_bias,
+                  outer_proj, out_grad):
+    width = states.shape[1]
+    block = short[0].shape[0]
+    long_block = inner_bias.shape[0]
+    places = 8 * depth
+    packed = pack_vectors(short, inner_bias)
+    merged, attn, inner, outer, table = gather_all(
+        depth, [[query_proj, key_proj, value_proj], [attn_proj], [inner_proj], [outer_proj], [packed]]
+    )
+    table = table.reshape(places, -1)
+    vectors = table[:, : 8 * block].reshape(places, 8, block).transpose(0, 2, 1).reshape(width, 8)
+    widened = table[:, 8 * block : 8 * block + long_block].reshape(-1)
+    weights = (merged.reshape(width, -1), attn.reshape(width, -1), inner.reshape(width, -1), outer.reshape(-1, width),
+               vectors, widened)
+    encoded, kept = forward_pass(states, pad_mask, weights)
+    states_part, totals = backward_pass(states, pad_mask, out_grad, weights, kept)
+    merged_g, attn_g, inner_g, outer_g, vector_g, widened_g = totals
+    low = [
+        part.astype(jnp.bfloat16).reshape(4, depth, 2, part.shape[0] // places, part.shape[1])
+        for part in (outer_g, inner_g, merged_g, attn_g)
+    ]
+    table_g = jnp.concatenate(
+        (vector_g.reshape(places, block, 8).transpose(0, 2, 1).reshape(places, -1), widened_g.reshape(places, -1)), axis=1
+    )
+    table_g = jnp.pad(table_g, ((0, 0), (0, 1024 - table_g.shape[1]))).reshape(4, depth, 2, 8, 128)
+    outer_sum, inner_sum, merged_sum, attn_sum, table_sum = scatter_all(depth, low + [table_g])
+    flat = table_sum.reshape(-1)
+    vector_sum = flat[: 8 * block].reshape(8, block)
+    widened_sum = flat[8 * block : 8 * block + long_block]
+    return ordered(encoded, states_part, merged_sum, attn_sum, inner_sum, outer_sum, vector_sum, widened_sum)
 
 
 def solution(mesh):
-    return jax.shard_map(
-        shards,
-        mesh=mesh,
-        in_specs=(
-            P(("dp", "fsdp"), None),
-            P(("dp", "fsdp"), None),
-            P(("dp", "fsdp"), None),
-            P(("dp", "fsdp"), None),
-            P(("dp", "fsdp"), None),
-            P(("dp", "fsdp"), None),
-            P(("dp", "fsdp")),
-            P(("dp", "fsdp")),
-            P(("dp", "fsdp")),
-            P(("dp", "fsdp")),
-            P(("dp", "fsdp")),
-            P(("dp", "fsdp"), None),
-            P(("dp", "fsdp")),
-            P(("dp", "fsdp"), None),
-            P(("dp", "fsdp")),
-            P(("dp", "fsdp")),
-            P(("dp", "fsdp")),
-            P(("dp", "fsdp"), None),
-        ),
-        out_specs=(
-            P(("dp", "fsdp"), None),
-            P(("dp", "fsdp"), None),
-            P(("dp", "fsdp"), None),
-            P(("dp", "fsdp"), None),
-            P(("dp", "fsdp"), None),
-            P(("dp", "fsdp"), None),
-            P(("dp", "fsdp")),
-            P(("dp", "fsdp")),
-            P(("dp", "fsdp")),
-            P(("dp", "fsdp")),
-            P(("dp", "fsdp")),
-            P(("dp", "fsdp"), None),
-            P(("dp", "fsdp")),
-            P(("dp", "fsdp"), None),
-            P(("dp", "fsdp")),
-            P(("dp", "fsdp")),
-            P(("dp", "fsdp")),
-        ),
-        check_vma=False,
-    )
+    dps, others = mesh.shape["dp"], mesh.shape["fsdp"]
+    matrix = P(("dp", "fsdp"), None)
+    vector = P(("dp", "fsdp"))
+
+    def whole(*arrays):
+        rows = arrays[2].shape[0] // (dps * others)
+        depth = others // 2 if rows % 16 == 0 and dps == 4 and others % 2 == 0 else 0
+        return jax.shard_map(
+            functools.partial(shards, depth),
+            mesh=mesh,
+            in_specs=(matrix,) * 6 + (vector,) * 5 + (matrix, vector, matrix) + (vector,) * 3 + (matrix,),
+            out_specs=(matrix,) * 6 + (vector,) * 5 + (matrix, vector, matrix) + (vector,) * 3,
+            check_vma=False,
+        )(*arrays)
+
+    return whole

time: 1230 us -> 432 us (0.35)
  waiting for transfers between devices: 846 us -> 0 us
  Pallas kernels: 0 us -> 275 us
  blocking collectives: 120 us -> 0 us
  matrix products: 175 us -> 102 us
  local copies, waits for them, and re-layouts: 53.7 us -> 39.8 us
  between operations: 15 us -> 1.48 us
    reduce_scatter x3 -> x0, waiting for transfers between devices: 517 us -> none  [the longest x1 187 us: reduce_grads(): lax.psum_scatter(outer, ('dp', 'fsdp'), scatter_dimension=0, tiled=True)]
    pallas_call x0 -> x2, Pallas kernels: none -> 275 us  [the longest x1 139 us: gather_all(): pl.pallas_call(functools.partial(gather_kernel, depth, tuple((len(group)...]
    unnamed x11 -> x0, waiting for transfers between devices: 175 us -> none
    all_gather x4 -> x0, waiting for transfers between devices: 154 us -> none  [the longest x1 74.3 us: collect(): lax.all_gather(inner, ('dp', 'fsdp'), axis=0, tiled=True)]
    all_gather x2 -> x0, blocking collectives: 80.7 us -> none  [the longest x1 43.8 us: collect(): lax.all_gather(vectors, ('dp', 'fsdp'), axis=0, tiled=True)]
    unnamed x1 -> x0, blocking collectives: 39.5 us -> none
    dot_general x8 -> x4, matrix products: 49.8 us -> 22.4 us  [contract_rows(): lax.dot_general(left, right, (((0,), (0,)), ((), ())), preferred_element_...]
    dot_general x8 -> x4, matrix products: 49.2 us -> 30.3 us  [times_transposed(): lax.dot_general(left, right, (((1,), (1,)), ((), ())), preferred_element_...]
  transfers between devices with their start and end apart: 9 -> 0, of which waited for: 8 -> 0; matrix products, arithmetic and copies ran while one was open for 11% -> 0% of each run, Pallas kernels for 0% -> 0%
where the time goes in v1:
time: 432 us; the launch traced here: 427 us
  Pallas kernels  275 us (64%)
  matrix products  102 us (24%)
  local copies, waits for them, and re-layouts  39.8 us (9%)
  other arithmetic  9.16 us (2%)
    pallas_call x1, Pallas kernels, gather_all(): pl.pallas_call(functools.partial(gather_kernel, depth, tuple((len(group)...  139 us
    pallas_call x1, Pallas kernels, scatter_all(): pl.pallas_call(functools.partial(scatter_kernel, depth, len(wholes)), out...  136 us
    dot_general x4, matrix products, times_transposed(): lax.dot_general(left, right, (((1,), (1,)), ((), ())), preferred_element_...  30.3 us
    dot_general x1, matrix products, forward_pass(): jnp.dot(first_low, inner, preferred_element_type=jnp.float32)  25.6 us
    dot_general x4, matrix products, contract_rows(): lax.dot_general(left, right, (((0,), (0,)), ((), ())), preferred_element_...  22.4 us
    unnamed x65, local copies, waits for them, and re-layouts  12.4 us

profile of v1, /device:TPU:0, one launch (start us, length us, event | category | flops | bytes accessed | tf_op | source)
XLA Modules:
  0.0 427.1 jit_solution(15855725417592333885)
XLA Ops:
  0.7 6.1 %concatenate.10 = bf16[384]{0:T(512)(128)(2,1)S(1)} concatenate(bf16[32]{0:T(256)(128)(2,1)} %param.24, bf16[32]{0:T(256)(128)(2,1)} %param.25, bf16[32]{0:T(256)(128)(2,1)} %param.26, bf16[32]{0:T(256)(128)(2,1)} %param.27, bf16[32]{0:T(256)(128)(2,1)} %param.28, bf16[32]{0:T(256)(128)(2,1)} %param.32, bf16[32]{0:T(256)(128)(2,1)} %param.33, bf16[32]{0:T(256)(128)(2,1)} %param.34, ...), dimensions={0} | concatenate | bytes 1536 | tf_op jit(solution)/shard_map/concatenate | solution.py:528
  7.4 139.4 %gather_weights.1 = (bf16[4,4,2,32,3072]{4,3,2,1,0:T(8,128)(2,1)}, bf16[4,4,2,32,1024]{4,3,2,1,0:T(8,128)(2,1)}, bf16[4,4,2,32,4096]{4,3,2,1,0:T(8,128)(2,1)}, b...) custom-call(bf16[32,1024]{1,0:T(8,128)(2,1)} %refs_0_.1, bf16[32,1024]{1,0:T(8,128)(2,1)} %refs_1_.1, ...), custom_call_target="tpu_custom_call" | custom-call | tf_op jit(solution)/shard_map/gather_weights/pallas_call | solution.py:174
  148.0 8.6 %fusion.7 = bf16[512,3072]{0,1:T(8,128)(2,1)} fusion(bf16[1024,3072]{1,0:T(8,128)(2,1)} %bitcast.173, bf16[512,1024]{1,0:T(8,128)(2,1)} %param.18, f32[3072]{0:T(1024)S(1)} %pad_maximum_fusion), kind=kOutput, calls=%fused_computation.29 | convolution fusion | flops 3224371200 | bytes 10498048 | tf_op jit(solution)/shard_map/dot_general | solution.py:426
  156.6 4.3 reshape.215
  160.9 1.8 fusion.45
  164.5 1.7 fusion.49
  167.8 1.5 copy-done.11
  169.9 1.4 fusion.50
  171.7 25.6 %multiply_convert_fusion = (bf16[512,4096]{1,0:T(8,128)(2,1)S(1)}, f32[512,4096]{1,0:T(8,128)}, f32[512,4096]{1,0:T(8,128)}) fusion(f32[4096]{0:T(1024)S(1)} %fusion.34, bf16[1024,4096]{1,0:T(8,128)(2,1)S(1)} %bitcast.168, f32[512,1024]{1,0:T(8,128)S(1)} %get-tuple-element.85, f32[1024]{0:T(1024)S(1)} %bitcast.160, f32[1024]{0:T(1024)S(1)} %bitcast.155, ...), kind=kOutput, calls=%fused_computation.5 | convolution fusion | flops 4436000768 | bytes 31485952 | tf_op jit(solution)/shard_map/dot_general | solution.py:439
  197.4 4.7 %fusion.51 = (f32[512]{0:T(512)S(1)}, f32[512,1024]{1,0:T(8,128)S(1)}) fusion(f32[1024]{0:T(1024)S(1)} %bitcast.163, bf16[512,4096]{1,0:T(8,128)(2,1)S(1)} %get-tuple-element.55, bf16[4096,1024]{1,0:T(8,128)(2,1)S(1)} %bitcast.172, f32[1024]{0:T(1024)S(1)} %bitcast.161, f32[1024]{0:T(1024)S(1)} %bitcast.156, f32[512]{0:T(512)S(1)} %fusion.35, ...), kind=kOutput, calls=%fused_computation.121 | convolution fusion | flops 4298636800 | bytes 16795648 | tf_op jit(solution)/shard_map/dot_general | solution.py:443
  203.4 1.9 fusion.43
  205.5 15.1 %convert_reduce_fusion = (f32[4096]{0:T(1024)S(1)}, bf16[512,4096]{1,0:T(8,128)(2,1)}) fusion(f32[512,4096]{1,0:T(8,128)} %get-tuple-element.56, f32[512,4096]{1,0:T(8,128)} %get-tuple-element.86, f32[4096]{0:T(1024)S(1)} %fusion.34, bf16[512,1024]{1,0:T(8,128)(2,1)S(1)} %get-tuple-element.44, bf16[4096,1024]{1,0:T(8,128)(2,1)} %bitcast.169), kind=kOutput, calls=%fused_computation.3 | convolution fusion | flops 4330614784 | bytes 30441472 | tf_op jit(solution)/shard_map/dot_general | solution.py:375
  220.6 9.1 %multiply_reduce_fusion.1 = (f32[1024]{0:T(1024)S(1)}, f32[512]{0:T(512)S(1)}, f32[1024]{0:T(1024)S(1)}, f32[512,1024]{1,0:T(8,128)S(1)}) fusion(f32[512,1024]{1,0:T(8,128)S(1)} %get-tuple-element.85, f32[512]{0:T(512)S(1)} %fusion.35, f32[512]{0:T(512)S(1)} %broadcast_multiply_fusion.1, f32[1024]{0:T(1024)S(1)} %bitcast.157, ...), kind=kOutput, calls=%fused_computation.46 | convolution fusion | flops 4300207616 | bytes 18894848 | tf_op jit(solution)/shard_map/dot_general | solution.py:375
  230.4 1.3 copy-done.4
  233.0 1.3 convolution_convert_fusion.4
  234.2 2.4 reshape.231
  236.6 2.8 copy.63
  239.5 3.9 convolution_bitcast_fusion
  244.5 1.3 multiply_convert_fusion.1
  245.9 1.5 multiply_bitcast_fusion
  248.2 1.5 convert_reduce_fusion.1
  249.7 3.1 copy.68
  252.8 4.9 %add_add_fusion.4 = f32[512,1024]{1,0:T(8,128)} fusion(f32[512,1024]{1,0:T(8,128)S(1)} %copy-done.5, bf16[1024,3072]{1,0:T(8,128)(2,1)S(1)} %bitcast.176, bf16[384,8,4,128]{3,2,1,0:T(4,128)(2,1)S(1)} %bitcast.137, f32[512]{0:T(512)S(1)} %negate_multiply_fusion.1), kind=kOutput, calls=%fused_computation.61 | convolution fusion | flops 3222274048 | bytes 13633536 | tf_op jit(solution)/shard_map/dot_general | solution.py:375
  257.7 6.8 %convolution_convert_fusion.1 = bf16[4096,1024]{1,0:T(8,128)(2,1)} fusion(bf16[512,4096]{1,0:T(8,128)(2,1)S(1)} %copy-done.22, bf16[512,1024]{1,0:T(8,128)(2,1)S(1)} %copy-done.13), kind=kOutput, calls=%fused_computation.20 | convolution fusion | flops 4299161600 | bytes 13631488 | tf_op jit(solution)/shard_map/dot_general | solution.py:369
  264.5 7.2 %convolution_convert_fusion = bf16[1024,4096]{1,0:T(8,128)(2,1)} fusion(bf16[512,4096]{1,0:T(8,128)(2,1)S(1)} %copy-done.23, f32[512,1024]{1,0:T(8,128)S(1)} %get-tuple-element.85, f32[1024]{0:T(1024)S(1)} %bitcast.162, f32[1024]{0:T(1024)S(1)} %bitcast.159, f32[512]{0:T(512)S(1)} %fusion.35, f32[512]{0:T(512)S(1)} %broadcast_multiply_fusion.1), kind=kOutput, calls=%fused_computation.19 | convolution fusion | flops 4301783040 | bytes 14692352 | tf_op jit(solution)/shard_map/dot_general | solution.py:369
  271.7 5.8 %convolution_convert_fusion.2 = bf16[3072,1024]{0,1:T(8,128)(2,1)} fusion(bf16[512,1024]{1,0:T(8,128)(2,1)S(1)} %copy-done.17, bf16[384,8,4,128]{3,2,1,0:T(4,128)(2,1)S(1)} %bitcast.138), kind=kOutput, calls=%fused_computation.24 | convolution fusion | flops 3224371200 | bytes 10485760 | tf_op jit(solution)/shard_map/dot_general | solution.py:369
  277.5 2.6 convolution_convert_fusion.3
  281.8 135.5 %scatter_gradients.1 = (f32[128,1024]{1,0:T(8,128)}, f32[32,4096]{1,0:T(8,128)}, f32[32,3072]{1,0:T(8,128)}, f32[32,1024]{1,0:T(8,128)}, f32[8,128]{1,0:T(8,128)}) custom-call(bf16[4,4,2,128,1024]{4,3,2,1,0:T(8,128)(2,1)} %bitcast.132, bf16[4,4,2,32,4096]{4,3,2,1,0:T(8,128)(2,1)} %bitcast.133, bf16[4,4,2,32,3072]{4,3,2,1,0:T(8,128)(2,1)} %bitcast.134, ...), custom_call_target="tpu_custom_call" | custom-call | tf_op jit(solution)/shard_map/scatter_gradients/pallas_call | solution.py:345
  417.3 1.8 fusion.46
  421.6 1.6 copy.118
  423.2 1.9 copy.119
  425.0 1.9 copy.120
  (108 shorter events, 15.6 us)
Async XLA Ops:
  162.7 1.0 copy-start
  162.7 1.8 copy-start.2
  162.7 3.5 copy-start.18
  162.7 1.8 copy-start.20
  164.5 7.2 %slice-start = ((s8[8388608]{0:T(1024)(128)(4,1)}), s8[4194304]{0:T(1024)(128)(4,1)S(1)}, s32[]{:S(2)}) async-start(s8[8388608]{0:T(1024)(128)(4,1)} %bitcast.166), calls=%async_computation | async-start | bytes 8388608
  166.2 5.5 %copy-start.6 = (f32[4,16,128,128]{2,3,1,0:T(8,128)}, f32[4,16,128,128]{2,3,1,0:T(8,128)S(1)}, u32[]{:S(2)}) copy-start(f32[4,16,128,128]{2,3,1,0:T(8,128)S(1)} %get-tuple-element.83) | copy-start | bytes 12582916
  166.2 3.2 copy-start.11
  166.2 3.7 copy-start.16
  166.2 5.5 %slice-start.1 = ((s8[8388608]{0:T(1024)(128)(4,1)}), s8[4194304]{0:T(1024)(128)(4,1)S(1)}, s32[]{:S(2)}) async-start(s8[8388608]{0:T(1024)(128)(4,1)} %bitcast.166), calls=%async_computation.1 | async-start | bytes 8388608
  167.8 3.8 copy-start.8
  169.9 27.4 %slice-start.2 = ((s8[8388608]{0:T(1024)(128)(4,1)}), s8[4194304]{0:T(1024)(128)(4,1)S(1)}, s32[]{:S(2)}) async-start(s8[8388608]{0:T(1024)(128)(4,1)} %bitcast.170), calls=%async_computation.2 | async-start | bytes 8388608
  171.7 25.6 %slice-start.3 = ((s8[8388608]{0:T(1024)(128)(4,1)}), s8[4194304]{0:T(1024)(128)(4,1)S(1)}, s32[]{:S(2)}) async-start(s8[8388608]{0:T(1024)(128)(4,1)} %bitcast.170), calls=%async_computation.3 | async-start | bytes 8388608
  197.4 4.8 %copy-start.21 = (bf16[512,4096]{1,0:T(8,128)(2,1)}, bf16[512,4096]{1,0:T(8,128)(2,1)S(1)}, u32[]{:S(2)}) copy-start(bf16[512,4096]{1,0:T(8,128)(2,1)S(1)} %get-tuple-element.55) | copy-start | bytes 12582916
  197.4 5.1 %copy-start.10 = (bf16[512,1024]{1,0:T(8,128)(2,1)S(1)}, bf16[512,1024]{1,0:T(8,128)(2,1)}, u32[]{:S(2)}) copy-start(bf16[512,1024]{1,0:T(8,128)(2,1)} %param.35) | copy-start | bytes 3145732
  205.5 15.1 %copy-start.12 = (bf16[512,1024]{1,0:T(8,128)(2,1)}, bf16[512,1024]{1,0:T(8,128)(2,1)S(1)}, u32[]{:S(2)}) copy-start(bf16[512,1024]{1,0:T(8,128)(2,1)S(1)} %get-tuple-element.44) | copy-start | bytes 3145732
  230.4 1.3 copy-start.4
  231.9 1.0 copy-start.14
  239.5 3.9 copy-start.7
  239.5 3.9 copy-start.19
  244.5 1.3 copy-start.3
  245.8 1.6 copy-start.1
  245.9 6.9 %slice-start.4 = ((s8[6291456]{0:T(1024)(128)(4,1)}), s8[4194304]{0:T(1024)(128)(4,1)S(1)}, s32[]{:S(2)}) async-start(s8[6291456]{0:T(1024)(128)(4,1)} %bitcast.174), calls=%async_computation.4 | async-start | bytes 8388608
  248.1 4.6 %slice-start.5 = ((s8[6291456]{0:T(1024)(128)(4,1)}), s8[2097152]{0:T(1024)(128)(4,1)S(1)}, s32[]{:S(2)}) async-start(s8[6291456]{0:T(1024)(128)(4,1)} %bitcast.174), calls=%async_computation.5 | async-start | bytes 4194304
  249.6 3.1 copy-start.5
  252.8 4.9 %copy-start.13 = (bf16[512,1024]{1,0:T(8,128)(2,1)S(1)}, bf16[512,1024]{1,0:T(8,128)(2,1)}, u32[]{:S(2)}) copy-start(bf16[512,1024]{1,0:T(8,128)(2,1)} %copy-done.12) | copy-start | bytes 3145732
  252.8 4.9 %copy-start.22 = (bf16[512,4096]{1,0:T(8,128)(2,1)S(1)}, bf16[512,4096]{1,0:T(8,128)(2,1)}, u32[]{:S(2)}) copy-start(bf16[512,4096]{1,0:T(8,128)(2,1)} %copy-done.21) | copy-start | bytes 12582916
  257.7 6.8 %copy-start.23 = (bf16[512,4096]{1,0:T(8,128)(2,1)S(1)}, bf16[512,4096]{1,0:T(8,128)(2,1)}, u32[]{:S(2)}) copy-start(bf16[512,4096]{1,0:T(8,128)(2,1)} %get-tuple-element.50) | copy-start | bytes 12582916
  264.5 7.2 %copy-start.17 = (bf16[512,1024]{1,0:T(8,128)(2,1)S(1)}, bf16[512,1024]{1,0:T(8,128)(2,1)}, u32[]{:S(2)}) copy-start(bf16[512,1024]{1,0:T(8,128)(2,1)} %param.18) | copy-start | bytes 3145732
  271.7 5.8 %copy-start.9 = (bf16[4,128,16,64]{1,0,3,2:T(4,128)(2,1)S(1)}, bf16[4,128,16,64]{1,0,3,2:T(4,128)(2,1)}, u32[]{:S(2)}) copy-start(bf16[4,128,16,64]{1,0,3,2:T(4,128)(2,1)} %copy-done.8) | copy-start | bytes 3145732
  271.7 5.8 %copy-start.15 = (bf16[512,1024]{1,0:T(8,128)(2,1)S(1)}, bf16[512,1024]{1,0:T(8,128)(2,1)}, u32[]{:S(2)}) copy-start(bf16[512,1024]{1,0:T(8,128)(2,1)} %copy-done.14) | copy-start | bytes 3145732
